TPU v7x, 512 devices: a whole 4x4x16 slice. The times are simulated.
512 devices in a mesh: tiles: 64 (over y, z), probe: 8 (over x, core).
Axes of the slice: x: 4, y: 4, z: 16, core: 2. Of those that a mesh axis runs over, the one named last changes fastest.
Arguments:
- coords: float32 [128, 2, 1024], P('tiles'), as said below
- noise_var: float32 [128, 1024], P('tiles'), may hold values from 0.25 to 1
- probes: float32 [128, 64, 1024], P('tiles', 'probe'), may hold values from -6 to 6
- pair_list: int32 [128, 4], P('tiles'), may hold values from -1 to 127, as said below
Outputs:
- solution: float32 [128, 64, 1024], P('tiles', 'probe')
- variance: float32 [128, 1024], P('tiles', 'probe')
Inputs may be any that keep to these rules, and one draw needn't show every extreme that they name: `coords`: tile t lies in one unit cell of a grid 2 cells wide: the tiles t with t // 2 = g occupy 2 of the cells of grid rows 2 g and 2 g + 1, in raster order; its points lie inside its cell, the first coordinate being the column. pair_list[t, k] is the tile in the cell right of, below-left of, below, and below-right of tile t's cell for k = 0, 1, 2, 3, or -1 where that cell holds no tile.
All inputs are finite; a program needn't handle non-finite values.
Results may differ from a plain program's by a relative error of at most 0.0004.
Values may be sent and summed in bfloat16 or wider, within the bound.
A program may use at most 64 MiB of HBM per device.

v0:
```python
import jax
import jax.numpy as jnp
from jax import lax
from jax.sharding import PartitionSpec as P

PROBES = 64
ITERS = 2


support = 0.5
batch_blocks = 2


def shifted(block, axis, distance):
    devices = range(lax.axis_size(axis))
    route = [(i - distance, i) for i in devices if i - distance in devices]
    return lax.ppermute(block, axis, route)


def kernel_weights(row_points, col_points):
    delta_x = row_points[:, 0, :, None] - col_points[:, 0, None, :]
    delta_y = row_points[:, 1, :, None] - col_points[:, 1, None, :]
    scaled = jnp.sqrt(delta_x * delta_x + delta_y * delta_y) / support
    return jnp.maximum(1.0 - scaled, 0.0) ** 4 * (4.0 * scaled + 1.0)


def prepare(left_idx, right_idx, live_int):
    live_float = live_int.astype(jnp.float32)
    return (left_idx, right_idx, live_float, left_idx.shape[0] // batch_blocks)


def pair_pass(running, left_points, left_field, right_points, right_field, layout, want_right):
    left_idx, right_idx, live_float, turn_count = layout

    def advance(number, current):
        first_slot = number * batch_blocks
        left_sel = lax.dynamic_slice_in_dim(left_idx, first_slot, batch_blocks)
        right_sel = lax.dynamic_slice_in_dim(right_idx, first_slot, batch_blocks)
        live_sel = lax.dynamic_slice_in_dim(live_float, first_slot, batch_blocks)
        weights = (
            kernel_weights(left_points[left_sel], right_points[right_sel]) * live_sel[:, None, None]
        )
        blocks = weights.astype(jnp.bfloat16)
        current = current.at[left_sel].add(
            jnp.einsum(
                "bij,bcj->bci", blocks, right_field[right_sel], preferred_element_type=jnp.float32
            )
        )
        if want_right:
            current = current.at[right_sel].add(
                jnp.einsum(
                    "bij,bci->bcj", blocks, left_field[left_sel], preferred_element_type=jnp.float32
                )
            )
        return current

    return lax.fori_loop(0, turn_count, advance, running)


def column_sums(left_part, right_part):
    return jnp.sum(left_part * right_part, axis=(0, 2))


def squares(vector):
    return lax.psum(column_sums(vector, vector), "tiles")


def shards(coords, noise_var, probes, pair_list):
    tile_count = coords.shape[0]
    device = lax.axis_index("tiles")
    offset = device * tile_count
    own_tiles = jnp.arange(tile_count, dtype=jnp.int32)
    slot_tiles = jnp.repeat(own_tiles, 4)
    partners = pair_list.reshape(-1)
    partner_live = (partners >= 0).astype(jnp.int32)
    partner_local = jnp.where(partners >= 0, partners - offset, 0)
    own_layout = prepare(slot_tiles, partner_local, partner_live)
    self_layout = prepare(own_tiles, own_tiles, jnp.ones((tile_count,), jnp.int32))
    next_points = shifted(coords, "tiles", -1)
    wide_points = jnp.concatenate([coords, next_points], 0)
    solution = jnp.zeros(probes.shape, jnp.float32)
    residual = probes
    direction = probes
    norm_now = squares(residual)
    for sweep_index in range(ITERS):
        vector_half = direction.astype(jnp.bfloat16)
        running = pair_pass(
            jnp.zeros(direction.shape, jnp.float32),
            coords,
            vector_half,
            coords,
            vector_half,
            self_layout,
            False,
        )
        next_field = shifted(vector_half, "tiles", -1)
        wide_field = jnp.concatenate([vector_half, next_field], 0)
        wide_terms = pair_pass(
            jnp.zeros((2 * tile_count,) + direction.shape[1:], jnp.float32),
            coords,
            vector_half,
            wide_points,
            wide_field,
            own_layout,
            True,
        )
        running = running + wide_terms[:tile_count]
        running = running + shifted(
            wide_terms[tile_count:].astype(jnp.bfloat16), "tiles", 1
        ).astype(jnp.float32)
        image_field = noise_var[:, None, :] * direction + running
        step_size = norm_now / lax.psum(column_sums(direction, image_field), "tiles")
        solution = solution + step_size[None, :, None] * direction
        residual = residual - step_size[None, :, None] * image_field
        norm_next = squares(residual)
        direction = residual + (norm_next / norm_now)[None, :, None] * direction
        norm_now = norm_next
    variance_term = jnp.sum(probes * solution, axis=1) / PROBES
    variance = lax.psum_scatter(variance_term, "probe", scatter_dimension=1, tiled=True)
    return (solution, variance)


def solution(mesh):
    in_specs = (
        P("tiles", None, None),
        P("tiles", None),
        P("tiles", "probe", None),
        P("tiles", None),
    )
    out_specs = (P("tiles", "probe", None), P("tiles", "probe"))
    return jax.shard_map(shards, mesh=mesh, in_specs=in_specs, out_specs=out_specs, check_vma=False)
```

profile of v0, /device:TPU:1, one launch (start us, length us, event | category | flops | bytes accessed | tf_op | source)
XLA Modules:
  0.0 638.3 jit_solution(6926133964639320319)
XLA Ops:
  7.2 0.8 convert_element_type.50
  8.1 1.3 collective-permute-start
  9.4 1.3 collective-permute-start.1
  10.7 0.7 convert_convert_fusion
  11.3 0.7 subtract_select_fusion
  12.0 1.3 gather_fusion.9
  13.4 0.7 constant_dynamic-update-slice_fusion.1
  14.9 0.8 collective-permute-done.1
  15.7 65.6 %while.40 = (s32[]{:T(128)}, f32[4,8,1024]{2,1,0:T(8,128)S(1)}, s32[8]{0:T(128)S(1)}, s32[8]{0:T(128)S(1)}, bf16[4,8,1024]{2,1,0:T(8,128)(2,1)S(1)}, /*index=5*/...) while((s32[]{:T(128)}, f32[4,8,1024]{2,1,0:T(8,128)S(1)}, ...), condition=%wide.region_5.6_spmd, body=%wide.region_2.0_spmd.sunk | while | flops 130058256 | bytes 991555 | solution.py:57
  17.8 6.3 fusion.58
  24.0 0.6 scatter_fusion
  25.2 6.3 fusion.59
  31.5 0.6 scatter_fusion.1
  34.1 6.3 fusion.58
  40.4 0.6 scatter_fusion
  41.6 6.3 fusion.59
  50.5 6.3 fusion.58
  56.8 0.6 scatter_fusion
  58.0 6.3 fusion.59
  66.9 6.3 fusion.58
  73.2 0.6 scatter_fusion
  74.4 6.3 fusion.59
  81.3 4.9 collective-permute-start.2
  86.2 6.0 fusion.21
  93.0 121.8 %all-reduce = (f32[8]{0:T(128)S(1)}, f32[8]{0:T(128)S(1)}) all-reduce(f32[8]{0:T(128)S(1)} %get-tuple-element.481, f32[8]{0:T(128)S(1)} %get-tuple-element.480), channel_id=1, replica_groups=mesh['tiles'=64,'probe'=8] {'tiles'}, use_global_device_ids=true, to_apply=%region_1.2 | all-reduce | flops 16 | bytes 128 | tf_op jit(solution)/shard_map/psum | solution.py:65
  215.0 110.1 %psum.30 = f32[8]{0:T(128)S(1)} all-reduce(f32[8]{0:T(128)S(1)} %multiply_reduce_fusion.2), channel_id=1, replica_groups=mesh['tiles'=64,'probe'=8] {'tiles'}, use_global_device_ids=true, to_apply=%region_10.11 | all-reduce | flops 8 | bytes 64 | tf_op jit(solution)/shard_map/psum | solution.py:65
  325.3 1.5 collective-permute-start.3
  327.3 2.7 collective-permute-done.3
  330.0 65.6 %while.41 = (s32[]{:T(128)}, f32[4,8,1024]{2,1,0:T(8,128)S(1)}, s32[8]{0:T(128)S(1)}, s32[8]{0:T(128)S(1)}, bf16[4,8,1024]{2,1,0:T(8,128)(2,1)S(1)}, /*index=5*/...) while((s32[]{:T(128)}, f32[4,8,1024]{2,1,0:T(8,128)S(1)}, ...), condition=%wide.region_14.0_spmd, body=%wide.region_11.14_spmd.sunk | while | flops 130058256 | bytes 991555 | solution.py:57
  332.0 6.3 fusion.64
  338.3 0.6 scatter_fusion.2
  339.5 6.3 fusion.65
  348.4 6.3 fusion.64
  354.7 0.6 scatter_fusion.2
  355.9 6.3 fusion.65
  364.8 6.3 fusion.64
  371.1 0.6 scatter_fusion.2
  372.3 6.3 fusion.65
  381.2 6.3 fusion.64
  387.5 0.6 scatter_fusion.2
  388.6 6.3 fusion.65
  395.6 3.4 collective-permute-start.4
  398.9 6.0 fusion.20
  405.7 110.5 %psum.31 = f32[8]{0:T(128)S(1)} all-reduce(f32[8]{0:T(128)S(1)} %multiply_reduce_fusion.1), channel_id=1, replica_groups=mesh['tiles'=64,'probe'=8] {'tiles'}, use_global_device_ids=true, to_apply=%region_17.0 | all-reduce | flops 8 | bytes 64 | tf_op jit(solution)/shard_map/psum | solution.py:112
  516.3 0.7 multiply_reduce_fusion
  517.0 1.0 copy.6
  518.0 111.9 %reduce-scatter.4.cloned.1.call-done = f32[128,2]{1,0:T(8,128)} async-done(((f32[1024,2]{1,0:T(8,128)}), f32[128,2]{1,0:T(8,128)}) %reduce-scatter.4.cloned.1.call-update) | async-done | bytes 1040
  630.0 1.5 copy.7
  (161 shorter events, 27.6 us)
Async XLA Ops:
  7.2 8.6 %copy-start.1 = (f32[2,2,1024]{2,1,0:T(2,128)S(1)}, f32[2,2,1024]{2,1,0:T(2,128)}, u32[]{:S(2)}) copy-start(f32[2,2,1024]{2,1,0:T(2,128)} %param.8) | copy-start | bytes 49156
  7.2 622.8 %reduce-scatter.4.cloned.1.call-start = ((), (), s32[]{:S(2)}) async-start(), calls=%async_computation.1 | async-start | bytes 589824
  8.1 7.6 %collective-permute-start = (bf16[2,8,1024]{2,1,0:T(8,128)(2,1)S(1)}, bf16[2,8,1024]{2,1,0:T(8,128)(2,1)S(1)}, u32[]{:S(2)}, u32[]{:S(2)}) collective-permute-start(bf16[2,8,1024]{2,1,0:T(8,128)(2,1)S(1)} %convert_element_type.50), channel_id=1, source_target_pairs={{8,0},{16,8},{24,16},{32,24},{40,32},{48,40},{56,48},{64,56},{72,6... | collective-permute-start | bytes 98312 | tf_op jit(solution)/shard_map/ppermute | solution.py:17
  9.4 6.3 collective-permute-start.1
  81.3 10.9 %collective-permute-start.2 = (bf16[2,8,1024]{2,1,0:T(8,128)(2,1)S(1)}, bf16[2,8,1024]{2,1,0:T(8,128)(2,1)S(1)}, u32[]{:S(2)}, u32[]{:S(2)}) collective-permute-start(bf16[2,8,1024]{2,1,0:T(8,128)(2,1)S(1)} %slice.155), channel_id=1, source_target_pairs={{0,8},{8,16},{16,24},{24,32},{32,40},{40,48},{48,56},{56,64},{64,7... | collective-permute-start | bytes 98312 | tf_op jit(solution)/shard_map/ppermute | solution.py:17
  86.2 6.0 copy-start
  86.2 6.0 copy-start.2
  325.3 4.7 collective-permute-start.3
  395.6 9.4 %collective-permute-start.4 = (bf16[2,8,1024]{2,1,0:T(8,128)(2,1)S(1)}, bf16[2,8,1024]{2,1,0:T(8,128)(2,1)S(1)}, u32[]{:S(2)}, u32[]{:S(2)}) collective-permute-start(bf16[2,8,1024]{2,1,0:T(8,128)(2,1)S(1)} %slice.154), channel_id=1, source_target_pairs={{0,8},{8,16},{16,24},{24,32},{32,40},{40,48},{48,56},{56,64},{64,7... | collective-permute-start | bytes 98312 | tf_op jit(solution)/shard_map/ppermute | solution.py:17
Sparse Core Ops, SparseCore 0:
  518.2 111.7 reduce-scatter.3
where the time goes:
time: 640 us; the launch traced here: 638 us
  blocking collectives  342 us (53%)
  waiting for transfers between devices  115 us (18%)
  matrix products  112 us (18%)
  local copies, waits for them, and re-layouts  25.1 us (4%)
  other arithmetic  15.5 us (2%)
  between operations  14.3 us (2%)
  starting transfers between devices  12.3 us (2%)
    psum x2, blocking collectives, squares(): return lax.psum(column_sums(vector, vector), 'tiles')  232 us
    unnamed x2, waiting for transfers between devices  112 us
    psum x1, blocking collectives, shards(): lax.psum(column_sums(direction, image_field), 'tiles')  111 us
    dot_general x10, matrix products, advance(): jnp.einsum('bij,bcj->bci', blocks, right_field[right_sel], preferred_elem...  62.3 us
    dot_general x8, matrix products, advance(): jnp.einsum('bij,bci->bcj', blocks, left_field[left_sel], preferred_elemen...  50.2 us
  transfers between devices with their start and end apart: 6, of which 3 were waited for; matrix products, arithmetic and copies ran while one was open for 3% of the time, Pallas kernels for 0%

commit v1 on v0

v1 whole, which is shorter than its diff:
```python
import functools
import jax
import jax.numpy as jnp
from jax import lax
from jax.experimental import pallas as pl
from jax.experimental.pallas import tpu as pltpu
from jax.sharding import PartitionSpec as P

F32 = jnp.float32
BF16 = jnp.bfloat16
MESH = pl.DeviceIdType.MESH

PTS = 1024
PROBES = 64
HALF = 8
CHIP = 16
NY, NZ, NX = 4, 16, 4
GROUPS = NY * NZ
LANES = 128
STRIPS = PTS // LANES

S_COORDS, S_Q, S_D, S_Z, S_ZX, S_AZ, S_AY, S_V = 0, 2, 7, 8, 11, 12, 27, 34
N_SEMS = 41


def fold(values):
    total = values[:, :LANES]
    for strip in range(1, STRIPS):
        total = total + values[:, strip * LANES : (strip + 1) * LANES]
    return total


def kernel(
    coords, noise, probes, pairs, sol, var,
    cbuf, lane, spread, nv, pv, qbuf, dbuf, qt, kbuf, zf, zb, zr, zx,
    az, ay, coef, vs, vr, lsem, ssem, rsem, s1, s2, s3,
):
    g = lax.axis_index("tiles")
    k = lax.axis_index("probe")
    y, z, x, c = g // NZ, lax.rem(g, NZ), k // 2, lax.rem(k, 2)
    other = 1 - c
    after, before = lax.rem(g + 1, GROUPS), lax.rem(g + GROUPS - 1, GROUPS)

    def at(dy=0, dz=0, dx=0, dc=0):
        return {
            "tiles": lax.rem(y + NY + dy, NY) * NZ + lax.rem(z + NZ + dz, NZ),
            "probe": lax.rem(x + NX + dx, NX) * 2 + lax.rem(c + dc, 2),
        }

    def signal(sem, device):
        pl.semaphore_signal(sem, inc=1, device_id=device, device_id_type=MESH)

    def copy(src, dst, index, device):
        return pltpu.make_async_remote_copy(
            src_ref=src, dst_ref=dst, send_sem=ssem.at[index], recv_sem=rsem.at[index],
            device_id=device, device_id_type=MESH,
        )

    loads = [
        pltpu.make_async_copy(src, dst, lsem.at[i])
        for i, (src, dst) in enumerate(((coords, cbuf.at[1]), (probes, pv), (noise, nv)))
    ]
    for load in loads:
        load.start()

    barrier = pltpu.get_barrier_semaphore()
    near = [
        {"tiles": after, "probe": k}, {"tiles": after, "probe": x * 2 + other},
        {"tiles": before, "probe": k}, {"tiles": before, "probe": x * 2 + other},
        at(dc=1), at(dz=1), at(dz=-1), at(dy=1), at(dy=-1), at(dx=1), at(dx=-1),
    ]
    for device in near:
        signal(barrier, device)

    def spread_rows(slot, tile):
        for axis in range(2):
            row = cbuf[1, tile, axis : axis + 1, :] * 8.0
            for b in range(STRIPS):
                cut = slice(b * LANES, (b + 1) * LANES)
                spread[slot, axis, cut, :] = jnp.broadcast_to(row[:, cut], (LANES, LANES)).T

    def fill(block, rows, cols):
        def step(r, carry):
            at_rows = pl.ds(pl.multiple_of(r * LANES, LANES), LANES)
            px, py = spread[rows, 0, at_rows, :], spread[rows, 1, at_rows, :]
            for b in range(STRIPS):
                cut = slice(b * LANES, (b + 1) * LANES)
                dx = px - lane[cols, 0:1, cut]
                dy = py - lane[cols, 1:2, cut]
                square = jnp.maximum(dx * dx + dy * dy, 1e-30)
                s4 = square * lax.rsqrt(square)
                m = jnp.maximum(4.0 - s4, 0.0)
                m = m * m
                kbuf[block, at_rows, cut] = ((m * m) * (s4 + 1.0)).astype(BF16)
            return carry

        lax.fori_loop(0, STRIPS, step, 0)

    def mul(field, block):
        return jnp.dot(field, kbuf[block], preferred_element_type=F32)

    def mul_t(field, block):
        return lax.dot_general(field, kbuf[block], (((1,), (1,)), ((), ())), preferred_element_type=F32)

    for load in loads:
        load.wait()
    qbuf[1, c] = pv[...].reshape(2 * HALF, PTS).astype(BF16)
    dbuf[c] = pv[c]
    lane[0] = cbuf[1, c] * 8.0
    spread_rows(0, c)
    fill(0, 0, 0)

    pl.semaphore_wait(barrier, len(near))
    sends = [
        copy(cbuf.at[1], cbuf.at[0], S_COORDS, near[0]),
        copy(cbuf.at[1], cbuf.at[2], S_COORDS + 1, near[2]),
        copy(qbuf.at[1, c], qbuf.at[1, c], S_Q, near[4]),
        copy(pv.at[other], dbuf.at[c], S_D, near[4]),
        copy(qbuf.at[1, c], qbuf.at[0, c], S_Q + 1, near[0]),
        copy(qbuf.at[1, c], qbuf.at[0, c], S_Q + 2, near[1]),
        copy(qbuf.at[1, c], qbuf.at[2, c], S_Q + 3, near[2]),
        copy(qbuf.at[1, c], qbuf.at[2, c], S_Q + 4, near[3]),
    ]
    for send in sends:
        send.start()
    for device in (at(dz=1), at(dz=-1), at(dy=-1), at(dx=-1), at(dc=1)):
        signal(s1, device)

    spread_rows(1, other)
    fill(1, 1, 0)

    def by_tile(group):
        first, second = qbuf[group, 0].astype(F32), qbuf[group, 1].astype(F32)
        return (
            jnp.concatenate([first[:HALF], second[:HALF]], 0),
            jnp.concatenate([first[HALF:], second[HALF:]], 0),
        )

    sends[2].wait_recv()
    t0, t1 = by_tile(1)
    qt[0] = jnp.where(c == 0, t0, t1).astype(BF16)
    qt[1] = jnp.where(c == 0, t1, t0).astype(BF16)
    zf[...] = mul(qt[0], 0) + mul(qt[1], 1)

    pl.semaphore_wait(s1, 5)
    for device in (at(dz=2), at(dz=-2), at(dc=1)):
        signal(s2, device)

    sends[0].wait_recv()
    sends[1].wait_recv()
    first_next = 2 * (g + 1)
    low = (pairs[c, 1] >= first_next) | (pairs[c, 2] >= first_next) | (pairs[c, 3] >= first_next)
    lane[1] = jnp.where(low, cbuf[2, c], cbuf[0, other]) * 8.0
    lane[2] = jnp.where(low, cbuf[2, other], cbuf[0, c]) * 8.0
    fill(2, 0, 1)

    pl.semaphore_wait(s2, 3)
    for device in (at(dz=4), at(dz=-4)):
        signal(s3, device)

    fill(3, 0, 2)
    for send in sends[4:]:
        send.wait_recv()
    p0, p1 = by_tile(0)
    n0, n1 = by_tile(2)
    qt[2] = jnp.where(low, jnp.where(c == 0, n0, n1), jnp.where(c == 0, p1, p0)).astype(BF16)
    qt[3] = jnp.where(low, jnp.where(c == 0, n1, n0), jnp.where(c == 0, p0, p1)).astype(BF16)
    sends[3].wait_recv()
    noise_row = nv[pl.ds(c, 1), :]
    start = dbuf[...].reshape(CHIP, PTS)
    image = noise_row * start + (zf[...] + mul_t(qt[2], 2) + mul_t(qt[3], 3)) * (1.0 / 256.0)
    zf[...] = image
    zb[...] = image.astype(BF16)

    fields = [
        copy(zb, zr.at[1], S_Z, near[2]),
        copy(zb, zr.at[2], S_Z + 1, near[1]),
        copy(zb, zr.at[0], S_Z + 2, near[4]),
        copy(zf.at[pl.ds(pl.multiple_of(other * HALF, HALF), HALF), :], zx, S_ZX, near[4]),
    ]
    for send in fields:
        send.start()
    second = mul(zb[...], 0)
    pl.semaphore_wait(s3, 2)
    fields[2].wait_recv()
    second = second + mul(zr[0], 1)
    fields[0].wait_recv()
    fields[1].wait_recv()
    across = jnp.where(low, zr[1].astype(F32), zr[2].astype(F32)).astype(BF16)
    second = second + 2.0 * mul_t(across, 2)
    second = second * (1.0 / 256.0) + noise_row * image

    moments = jnp.concatenate(
        [fold(start * start), fold(start * image), fold(image * image), fold(image * second), jnp.zeros((64, LANES), F32)], 0
    )
    az[0] = jnp.sum(moments.T, axis=0, keepdims=True)
    along_z = [copy(az.at[0], az.at[d], S_AZ + d - 1, at(dz=d)) for d in range(1, NZ)]
    for d in (8, 7, 9, 6, 10, 5, 11, 4, 12, 3, 13, 2, 14, 1, 15):
        along_z[d - 1].start()
    for send in along_z:
        send.wait_recv()
    ay[0] = jnp.sum(az[...], axis=0)
    steps = [(dy, dc) for dy in range(NY) for dc in range(2)][1:]
    along_y = [copy(ay.at[0], ay.at[j + 1], S_AY + j, at(dy=dy, dc=dc)) for j, (dy, dc) in enumerate(steps)]
    for j in (3, 4, 1, 2, 5, 6, 0):
        along_y[j].start()
    for send in along_y:
        send.wait_recv()
    m0 = jnp.sum(ay[...], axis=0)
    m1, m2, m3 = (pltpu.roll(m0, LANES - CHIP * i, 1) for i in (1, 2, 3))
    step0 = m0 / m1
    growth = m2 / m1
    step1 = (m2 - m1 * m1 / m0) / (m3 - m2 * growth)
    for i, value in enumerate((step0 + step0 * step1 * growth, -step0 * step1)):
        coef[i] = jnp.broadcast_to(value, (LANES, LANES)).T

    mine = pl.ds(pl.multiple_of(c * HALF, HALF), HALF)
    alpha = jnp.concatenate([coef[0, mine, :]] * STRIPS, 1)
    beta = jnp.concatenate([coef[1, mine, :]] * STRIPS, 1)
    fields[3].wait_recv()
    for tile, held in ((c, zf[mine, :]), (other, zx[...])):
        begin = pv[tile]
        result = alpha * begin + beta * held
        sol[tile] = result
        total = jnp.sum(begin * result, axis=0, keepdims=True) * (1.0 / PROBES)
        for j in range(STRIPS):
            vs[j, pl.ds(tile, 1), :] = total[:, j * LANES : (j + 1) * LANES]
    across_x = []
    for j, (dx, dc) in enumerate([(dx, dc) for dx in range(NX) for dc in range(2)][1:]):
        device = at(dx=dx, dc=dc)
        across_x.append(copy(vs.at[device["probe"]], vr.at[j], S_V + j, device))
    for send in across_x:
        send.start()
    for send in across_x:
        send.wait_recv()
    var[...] = vs[k] + jnp.sum(vr[...], axis=0)
    for send in sends + fields + along_z + along_y + across_x:
        send.wait_send()


def shards(coords, noise_var, probes, pair_list):
    anywhere = pl.BlockSpec(memory_space=pl.ANY)
    return pl.pallas_call(
        kernel,
        out_shape=(
            jax.ShapeDtypeStruct(probes.shape, F32),
            jax.ShapeDtypeStruct((2, LANES), F32),
        ),
        in_specs=[anywhere, anywhere, anywhere, pl.BlockSpec(memory_space=pltpu.SMEM)],
        out_specs=[pl.BlockSpec(memory_space=pltpu.VMEM)] * 2,
        scratch_shapes=[
            pltpu.VMEM((3, 2, 2, PTS), F32),
            pltpu.VMEM((3, 2, PTS), F32),
            pltpu.VMEM((2, 2, PTS, LANES), F32),
            pltpu.VMEM((2, PTS), F32),
            pltpu.VMEM((2, HALF, PTS), F32),
            pltpu.VMEM((3, 2, 2 * HALF, PTS), BF16),
            pltpu.VMEM((2, HALF, PTS), F32),
            pltpu.VMEM((4, CHIP, PTS), BF16),
            pltpu.VMEM((4, PTS, PTS), BF16),
            pltpu.VMEM((CHIP, PTS), F32),
            pltpu.VMEM((CHIP, PTS), BF16),
            pltpu.VMEM((3, CHIP, PTS), BF16),
            pltpu.VMEM((HALF, PTS), F32),
            pltpu.VMEM((NZ, 1, LANES), F32),
            pltpu.VMEM((8, 1, LANES), F32),
            pltpu.VMEM((2, LANES, LANES), F32),
            pltpu.VMEM((8, 2, LANES), F32),
            pltpu.VMEM((7, 2, LANES), F32),
            pltpu.SemaphoreType.DMA((3,)),
            pltpu.SemaphoreType.DMA((N_SEMS,)),
            pltpu.SemaphoreType.DMA((N_SEMS,)),
            pltpu.SemaphoreType.REGULAR,
            pltpu.SemaphoreType.REGULAR,
            pltpu.SemaphoreType.REGULAR,
        ],
        compiler_params=pltpu.CompilerParams(
            collective_id=0, has_side_effects=True, vmem_limit_bytes=32 << 20
        ),
    )(coords, noise_var, probes, pair_list)


def solution(mesh):
    in_specs = (
        P("tiles", None, None),
        P("tiles", None),
        P("tiles", "probe", None),
        P("tiles", None),
    )
    out_specs = (P("tiles", "probe", None), P("tiles", "probe"))
    return jax.shard_map(shards, mesh=mesh, in_specs=in_specs, out_specs=out_specs, check_vma=False)
```

time: 640 us -> 48.2 us (0.08)
  blocking collectives: 342 us -> 0 us
  waiting for transfers between devices: 115 us -> 0 us
  matrix products: 112 us -> 0 us
  Pallas kernels: 0 us -> 43.2 us
  local copies, waits for them, and re-layouts: 25.1 us -> 4.12 us
  other arithmetic: 15.5 us -> 0 us
  between operations: 14.3 us -> 0.65 us
  starting transfers between devices: 12.3 us -> 0 us
    psum x3 -> x0, blocking collectives: 342 us -> none  [the longest x2 232 us: squares(): return lax.psum(column_sums(vector, vector), 'tiles')]
    dot_general x18 -> x0, matrix products: 112 us -> none  [the longest x10 62.3 us: advance(): jnp.einsum('bij,bcj->bci', blocks, right_field[right_sel], preferred_elem...]
    unnamed x2 -> x0, waiting for transfers between devices: 112 us -> none
    pallas_call x0 -> x1, Pallas kernels: none -> 43.2 us  [shards(): pl.pallas_call(kernel, out_shape=(jax.ShapeDtypeStruct(probes.shape, F32)...]
    gather x35 -> x0, local copies, waits for them, and re-layouts: 20.4 us -> none  [the longest x9 5.92 us: advance(): left_points[left_sel]]
    ppermute x5 -> x0, starting transfers between devices: 12.3 us -> none  [shifted(): return lax.ppermute(block, axis, route)]
    scatter-add x18 -> x0, other arithmetic: 11.2 us -> none  [the longest x10 6.22 us: advance(): current.at[left_sel]]
  transfers between devices with their start and end apart: 6 -> 0, of which waited for: 3 -> 0; matrix products, arithmetic and copies ran while one was open for 3% -> 0% of each run, Pallas kernels for 0% -> 0%
where the time goes in v1:
time: 48.2 us; the launch traced here: 48 us
  Pallas kernels  43.2 us (90%)
  local copies, waits for them, and re-layouts  4.12 us (9%)
  between operations  0.65 us (1%)
    pallas_call x1, Pallas kernels, shards(): pl.pallas_call(kernel, out_shape=(jax.ShapeDtypeStruct(probes.shape, F32)...  43.2 us
    unnamed x10, local copies, waits for them, and re-layouts  4.12 us

profile of v1, /device:TPU:1, one launch (start us, length us, event | category | flops | bytes accessed | tf_op | source)
XLA Modules:
  0.0 48.0 jit_solution(7280798605755663610)
XLA Ops:
  0.6 0.0 copy-start
  0.6 0.8 %copy-done = f32[2,8,1024]{2,1,0:T(8,128)S(1)} copy-done((f32[2,8,1024]{2,1,0:T(8,128)S(1)}, f32[2,8,1024]{2,1,0:T(8,128)}, u32[]{:S(2)}) %copy-start) | copy-done | bytes 65560
  1.5 0.0 copy-start.1
  1.5 0.7 %copy-done.1 = f32[2,2,1024]{2,1,0:T(2,128)S(1)} copy-done((f32[2,2,1024]{2,1,0:T(2,128)S(1)}, f32[2,2,1024]{2,1,0:T(2,128)}, u32[]{:S(2)}) %copy-start.1) | copy-done | bytes 16408
  2.2 0.0 copy-start.2
  2.2 0.7 %copy-done.2 = f32[2,1024]{1,0:T(2,128)S(1)} copy-done((f32[2,1024]{1,0:T(2,128)S(1)}, f32[2,1024]{1,0:T(2,128)}, u32[]{:S(2)}) %copy-start.2) | copy-done | bytes 8216
  2.9 0.0 copy-start.3
  2.9 0.7 %copy-done.3 = s32[2,4]{1,0:T(2,128)S(1)} copy-done((s32[2,4]{1,0:T(2,128)S(1)}, s32[2,4]{1,0:T(2,128)}, u32[]{:S(2)}) %copy-start.3) | copy-done | bytes 56
  3.6 43.2 %shard_map.59 = (f32[2,8,1024]{2,1,0:T(8,128)S(1)}, f32[2,128]{1,0:T(2,128)S(1)}) custom-call(f32[2,2,1024]{2,1,0:T(2,128)S(1)} %copy-done.1, f32[2,1024]{1,0:T(2,128)S(1)} %copy-done.2, f32[2,8,1024]{2,1,0:T(8,128)S(1)} %copy-done, s32[2,4]{1,0:T(2,128)S(1)} %copy-done.3), custom_call_target="tpu_custom_call" | custom-call | tf_op jit(solution)/shard_map/pallas_call | solution.py:243
  46.8 0.6 %copy.8 = f32[2,8,1024]{2,1,0:T(8,128)} copy(f32[2,8,1024]{2,1,0:T(8,128)S(1)} %get-tuple-element.4) | data formatting | bytes 131072
  47.4 0.6 %copy.9 = f32[2,128]{1,0:T(2,128)} copy(f32[2,128]{1,0:T(2,128)S(1)} %get-tuple-element.5) | data formatting | bytes 2048
Async XLA Ops:
  0.6 0.8 %copy-start = (f32[2,8,1024]{2,1,0:T(8,128)S(1)}, f32[2,8,1024]{2,1,0:T(8,128)}, u32[]{:S(2)}) copy-start(f32[2,8,1024]{2,1,0:T(8,128)} %probes.1) | copy-start | bytes 196612
  1.5 0.7 %copy-start.1 = (f32[2,2,1024]{2,1,0:T(2,128)S(1)}, f32[2,2,1024]{2,1,0:T(2,128)}, u32[]{:S(2)}) copy-start(f32[2,2,1024]{2,1,0:T(2,128)} %coords.1) | copy-start | bytes 49156
  2.2 0.7 %copy-start.2 = (f32[2,1024]{1,0:T(2,128)S(1)}, f32[2,1024]{1,0:T(2,128)}, u32[]{:S(2)}) copy-start(f32[2,1024]{1,0:T(2,128)} %noise.1) | copy-start | bytes 24580
  2.9 0.7 %copy-start.3 = (s32[2,4]{1,0:T(2,128)S(1)}, s32[2,4]{1,0:T(2,128)}, u32[]{:S(2)}) copy-start(s32[2,4]{1,0:T(2,128)} %pairs.1) | copy-start | bytes 100

commit v2 on v1

v2 whole, which is shorter than its diff:
```python
import functools
import jax
import jax.numpy as jnp
from jax import lax
from jax.experimental import pallas as pl
from jax.experimental.pallas import tpu as pltpu
from jax.sharding import PartitionSpec as P

F32 = jnp.float32
BF16 = jnp.bfloat16
MESH = pl.DeviceIdType.MESH

PTS = 1024
PROBES = 64
HALF = 8
CHIP = 16
NY, NZ, NX = 4, 16, 4
GROUPS = NY * NZ
LANES = 128
STRIPS = PTS // LANES

S_COORDS, S_Q, S_D, S_Z, S_ZX, S_P, S_AZ, S_AY = 0, 2, 7, 8, 11, 12, 19, 50
N_SEMS = 65


def fold(values):
    total = values[:, :LANES]
    for strip in range(1, STRIPS):
        total = total + values[:, strip * LANES : (strip + 1) * LANES]
    return total


def kernel(
    coords, noise, probes, pairs, sol, var,
    cbuf, lane, spread, nv, pv, qbuf, dbuf, qt, k_self, k_pair, k_near, k_far, zf, zb, zr, zx,
    az, ay, coef, ps, pr, lsem, ssem, rsem, s1, s2, s3,
):
    g = lax.axis_index("tiles")
    k = lax.axis_index("probe")
    y, z, x, c = g // NZ, lax.rem(g, NZ), k // 2, lax.rem(k, 2)
    other = 1 - c
    after, before = lax.rem(g + 1, GROUPS), lax.rem(g + GROUPS - 1, GROUPS)

    def at(dy=0, dz=0, dx=0, dc=0):
        return {
            "tiles": lax.rem(y + NY + dy, NY) * NZ + lax.rem(z + NZ + dz, NZ),
            "probe": lax.rem(x + NX + dx, NX) * 2 + lax.rem(c + dc, 2),
        }

    def signal(sem, device):
        pl.semaphore_signal(sem, inc=1, device_id=device, device_id_type=MESH)

    def copy(src, dst, index, device):
        return pltpu.make_async_remote_copy(
            src_ref=src, dst_ref=dst, send_sem=ssem.at[index], recv_sem=rsem.at[index],
            device_id=device, device_id_type=MESH,
        )

    loads = [
        pltpu.make_async_copy(src, dst, lsem.at[i])
        for i, (src, dst) in enumerate(((coords, cbuf.at[1]), (probes, pv), (noise, nv)))
    ]
    for load in loads:
        load.start()

    barrier = pltpu.get_barrier_semaphore()
    near = [
        {"tiles": after, "probe": k}, {"tiles": after, "probe": x * 2 + other},
        {"tiles": before, "probe": k}, {"tiles": before, "probe": x * 2 + other},
        at(dc=1), at(dz=1), at(dz=-1), at(dz=1, dc=1), at(dz=-1, dc=1),
        at(dy=1), at(dy=-1), at(dx=1), at(dx=-1),
    ]
    for device in near:
        signal(barrier, device)

    def fill(block, cols, low=0, high=STRIPS):
        def step(r, carry):
            at_rows = pl.ds(pl.multiple_of(r * LANES, LANES), LANES)
            px, py = spread[0, at_rows, :], spread[1, at_rows, :]
            for b in range(STRIPS):
                cut = slice(b * LANES, (b + 1) * LANES)
                dx = px - lane[cols, 0:1, cut]
                dy = py - lane[cols, 1:2, cut]
                square = jnp.maximum(dx * dx + dy * dy, 1e-30)
                s4 = square * lax.rsqrt(square)
                m = jnp.maximum(4.0 - s4, 0.0)
                m = m * m
                block[at_rows, cut] = ((m * m) * (s4 + 1.0)).astype(BF16)
            return carry

        lax.fori_loop(low, high, step, 0)

    def times_rows(field, block):
        return lax.dot_general(
            field[...], block[...], (((1,), (1,)), ((), ())), preferred_element_type=F32
        )

    def times(field, block):
        return jnp.dot(field[...], block[...], preferred_element_type=F32)

    for load in loads:
        load.wait()
    lane[0] = cbuf[1, c] * 8.0
    for axis in range(2):
        for b in range(STRIPS):
            cut = slice(b * LANES, (b + 1) * LANES)
            spread[axis, cut, :] = jnp.broadcast_to(lane[0, axis : axis + 1, cut], (LANES, LANES)).T
    qbuf[1, c] = pv[...].reshape(2 * HALF, PTS).astype(BF16)
    dbuf[c] = pv[c]
    lane[1] = cbuf[1, other] * 8.0
    fill(k_self, 0, 0, 3)

    pl.semaphore_wait(barrier, len(near))
    sends = [
        copy(cbuf.at[1], cbuf.at[0], S_COORDS, near[0]),
        copy(cbuf.at[1], cbuf.at[2], S_COORDS + 1, near[2]),
        copy(qbuf.at[1, c], qbuf.at[1, c], S_Q, near[4]),
        copy(pv.at[other], dbuf.at[c], S_D, near[4]),
        copy(qbuf.at[1, c], qbuf.at[0, c], S_Q + 1, near[0]),
        copy(qbuf.at[1, c], qbuf.at[0, c], S_Q + 2, near[1]),
        copy(qbuf.at[1, c], qbuf.at[2, c], S_Q + 3, near[2]),
        copy(qbuf.at[1, c], qbuf.at[2, c], S_Q + 4, near[3]),
    ]
    for send in sends:
        send.start()
    for device in (at(dz=1), at(dz=-1), at(dy=-1), at(dx=-1), at(dx=1)):
        signal(s1, device)

    fill(k_self, 0, 3)
    fill(k_pair, 1)

    def by_tile(group):
        first, second = qbuf[group, 0].astype(F32), qbuf[group, 1].astype(F32)
        return (
            jnp.concatenate([first[:HALF], second[:HALF]], 0),
            jnp.concatenate([first[HALF:], second[HALF:]], 0),
        )

    pl.semaphore_wait(s1, 5)
    for device in (at(dz=2), at(dz=-2), at(dx=-1), at(dx=1)):
        signal(s2, device)
    sends[2].wait_recv()
    t0, t1 = by_tile(1)
    qt[0] = jnp.where(c == 0, t0, t1).astype(BF16)
    qt[1] = jnp.where(c == 0, t1, t0).astype(BF16)
    zf[...] = times(qt.at[0], k_self) + times_rows(qt.at[1], k_pair)

    sends[0].wait_recv()
    sends[1].wait_recv()
    first_next = 2 * (g + 1)
    low = (pairs[c, 1] >= first_next) | (pairs[c, 2] >= first_next) | (pairs[c, 3] >= first_next)
    lane[2] = jnp.where(low, cbuf[2, c], cbuf[0, other]) * 8.0
    lane[3] = jnp.where(low, cbuf[2, other], cbuf[0, c]) * 8.0
    fill(k_near, 2)

    pl.semaphore_wait(s2, 4)
    for device in (at(dz=4), at(dz=-4), at(dx=-1)):
        signal(s3, device)
    fill(k_far, 3)
    for send in sends[4:]:
        send.wait_recv()
    p0, p1 = by_tile(0)
    n0, n1 = by_tile(2)
    qt[2] = jnp.where(low, jnp.where(c == 0, n0, n1), jnp.where(c == 0, p1, p0)).astype(BF16)
    qt[3] = jnp.where(low, jnp.where(c == 0, n1, n0), jnp.where(c == 0, p0, p1)).astype(BF16)
    sends[3].wait_recv()
    noise_row = nv[pl.ds(c, 1), :]
    start = dbuf[...].reshape(CHIP, PTS)
    image = zf[...] + times_rows(qt.at[2], k_near) + times_rows(qt.at[3], k_far)
    image = noise_row * start + image * (1.0 / 256.0)
    zf[...] = image
    zb[...] = image.astype(BF16)

    fields = [
        copy(zb, zr.at[1], S_Z, near[2]),
        copy(zb, zr.at[2], S_Z + 1, near[1]),
        copy(zb, zr.at[0], S_Z + 2, near[4]),
        copy(zf.at[pl.ds(pl.multiple_of(other * HALF, HALF), HALF), :], zx, S_ZX, near[4]),
    ]
    for send in fields:
        send.start()
    products = (start * start, start * image)
    for j in range(STRIPS):
        for i in range(2):
            ps[j, i] = products[i][:, j * LANES : (j + 1) * LANES]
    shares = []
    for j, (dx, dc) in enumerate([(dx, dc) for dx in range(NX) for dc in range(2)][1:]):
        device = at(dx=dx, dc=dc)
        shares.append(copy(ps.at[device["probe"]], pr.at[j], S_P + j, device))
    for send in shares:
        send.start()

    moments = [fold(products[0]), fold(products[1]), fold(image * image)]
    square = fold(image * (times(zb, k_self) * (1.0 / 256.0) + noise_row * image))
    to_pair, to_near = times(zb, k_pair), times(zb, k_near)
    pl.semaphore_wait(s3, 3)
    fields[2].wait_recv()
    square = square + fold(to_pair * zr[0].astype(F32)) * (1.0 / 256.0)
    fields[0].wait_recv()
    fields[1].wait_recv()
    across = jnp.where(low, zr[1].astype(F32), zr[2].astype(F32))
    square = square + fold(to_near * across) * (2.0 / 256.0)

    table = jnp.concatenate(moments + [square, jnp.zeros((64, LANES), F32)], 0)
    az[0] = jnp.sum(table.T, axis=0, keepdims=True)
    along_z = [copy(az.at[0], az.at[i], S_AZ + i - 1, at(dz=i // 2, dc=i % 2)) for i in range(1, 2 * NZ)]
    for i in sorted(range(1, 2 * NZ), key=lambda i: -min(i // 2, NZ - i // 2)):
        along_z[i - 1].start()
    for send in along_z:
        send.wait_recv()
    ay[0] = jnp.sum(az[...], axis=0)
    plane = [copy(ay.at[0], ay.at[i], S_AY + i - 1, at(dx=i // NY, dy=i % NY)) for i in range(1, NX * NY)]
    for i in sorted(range(1, NX * NY), key=lambda i: -(min(i // NY, NX - i // NY) + min(i % NY, NY - i % NY))):
        plane[i - 1].start()
    for send in plane:
        send.wait_recv()
    m0 = jnp.concatenate([jnp.sum(ay[NY * i : NY * (i + 1)], axis=0) for i in range(NX)], 0)
    m1, m2, m3 = (pltpu.roll(m0, LANES - CHIP * i, 1) for i in (1, 2, 3))
    step0 = m0 / m1
    growth = m2 / m1
    step1 = (m2 - m1 * m1 / m0) / (m3 - m2 * growth)
    alpha, beta = step0 + step0 * step1 * growth, -step0 * step1
    at_lane = lax.broadcasted_iota(jnp.int32, (1, LANES), 1)
    packed = jnp.zeros((1, LANES), F32)
    for i in range(NX):
        for h, value in enumerate((alpha, beta)):
            first = 32 * i + CHIP * h
            row = value[i : i + 1]
            if first:
                row = pltpu.roll(row, first, 1)
            packed = jnp.where((at_lane >= first) & (at_lane < first + CHIP), row, packed)
    coef[...] = jnp.broadcast_to(packed, (LANES, LANES)).T

    mine = pl.ds(pl.multiple_of(c * HALF, HALF), HALF)
    alpha_mine = jnp.concatenate([coef[mine, :]] * STRIPS, 1)
    beta_mine = jnp.concatenate([coef[pl.ds(pl.multiple_of(CHIP + c * HALF, HALF), HALF), :]] * STRIPS, 1)
    fields[3].wait_recv()
    sol[c] = alpha_mine * pv[c] + beta_mine * zf[mine, :]
    sol[other] = alpha_mine * pv[other] + beta_mine * zx[...]
    for send in shares:
        send.wait_recv()
    for dc, tile in ((0, c), (1, other)):
        total = jnp.zeros((CHIP, LANES), F32)
        for dx in range(NX):
            share = ps.at[k] if (dx, dc) == (0, 0) else pr.at[2 * dx + dc - 1]
            total = total + coef[32 * dx : 32 * dx + CHIP, :] * share[0]
            total = total + coef[32 * dx + CHIP : 32 * dx + 2 * CHIP, :] * share[1]
        var[pl.ds(tile, 1), :] = jnp.sum(total, axis=0, keepdims=True) * (1.0 / PROBES)
    for send in sends + fields + shares + along_z + plane:
        send.wait_send()


def shards(coords, noise_var, probes, pair_list):
    anywhere = pl.BlockSpec(memory_space=pl.ANY)
    return pl.pallas_call(
        kernel,
        out_shape=(
            jax.ShapeDtypeStruct(probes.shape, F32),
            jax.ShapeDtypeStruct((2, LANES), F32),
        ),
        in_specs=[anywhere, anywhere, anywhere, pl.BlockSpec(memory_space=pltpu.SMEM)],
        out_specs=[pl.BlockSpec(memory_space=pltpu.VMEM)] * 2,
        scratch_shapes=[
            pltpu.VMEM((3, 2, 2, PTS), F32),
            pltpu.VMEM((4, 2, PTS), F32),
            pltpu.VMEM((2, PTS, LANES), F32),
            pltpu.VMEM((2, PTS), F32),
            pltpu.VMEM((2, HALF, PTS), F32),
            pltpu.VMEM((3, 2, 2 * HALF, PTS), BF16),
            pltpu.VMEM((2, HALF, PTS), F32),
            pltpu.VMEM((4, CHIP, PTS), BF16),
            pltpu.VMEM((PTS, PTS), BF16),
            pltpu.VMEM((PTS, PTS), BF16),
            pltpu.VMEM((PTS, PTS), BF16),
            pltpu.VMEM((PTS, PTS), BF16),
            pltpu.VMEM((CHIP, PTS), F32),
            pltpu.VMEM((CHIP, PTS), BF16),
            pltpu.VMEM((3, CHIP, PTS), BF16),
            pltpu.VMEM((HALF, PTS), F32),
            pltpu.VMEM((2 * NZ, 1, LANES), F32),
            pltpu.VMEM((NX * NY, 1, LANES), F32),
            pltpu.VMEM((LANES, LANES), F32),
            pltpu.VMEM((8, 2, CHIP, LANES), F32),
            pltpu.VMEM((7, 2, CHIP, LANES), F32),
            pltpu.SemaphoreType.DMA((3,)),
            pltpu.SemaphoreType.DMA((N_SEMS,)),
            pltpu.SemaphoreType.DMA((N_SEMS,)),
            pltpu.SemaphoreType.REGULAR,
            pltpu.SemaphoreType.REGULAR,
            pltpu.SemaphoreType.REGULAR,
        ],
        compiler_params=pltpu.CompilerParams(
            collective_id=0, has_side_effects=True, vmem_limit_bytes=32 << 20
        ),
    )(*(pltpu.with_memory_space_constraint(v, pltpu.MemorySpace.HBM) for v in (coords, noise_var, probes, pair_list)))


def solution(mesh):
    in_specs = (
        P("tiles", None, None),
        P("tiles", None),
        P("tiles", "probe", None),
        P("tiles", None),
    )
    out_specs = (P("tiles", "probe", None), P("tiles", "probe"))
    return jax.shard_map(shards, mesh=mesh, in_specs=in_specs, out_specs=out_specs, check_vma=False)
```

time: 48.2 us -> 42.6 us (0.88)
  local copies, waits for them, and re-layouts: 4.12 us -> 1.19 us
  Pallas kernels: 43.2 us -> 40.5 us
    unnamed x10 -> x2, local copies, waits for them, and re-layouts: 4.12 us -> 1.19 us
    pallas_call x1, Pallas kernels: 43.2 us -> 40.5 us  [shards(): pl.pallas_call(kernel, out_shape=(jax.ShapeDtypeStruct(probes.shape, F32)...]
where the time goes in v2:
time: 42.6 us; the launch traced here: 42.4 us
  Pallas kernels  40.5 us (95%)
  local copies, waits for them, and re-layouts  1.19 us (3%)
  between operations  0.64 us (2%)
    pallas_call x1, Pallas kernels, shards(): pl.pallas_call(kernel, out_shape=(jax.ShapeDtypeStruct(probes.shape, F32)...  40.5 us
    unnamed x2, local copies, waits for them, and re-layouts  1.19 us

profile of v2, /device:TPU:1, one launch (start us, length us, event | category | flops | bytes accessed | tf_op | source)
XLA Modules:
  0.0 42.4 jit_solution(5706287743521196130)
XLA Ops:
  0.6 40.5 %shard_map.59 = (f32[2,8,1024]{2,1,0:T(8,128)S(1)}, f32[2,128]{1,0:T(2,128)S(1)}) custom-call(f32[2,2,1024]{2,1,0:T(2,128)} %coords.1, f32[2,1024]{1,0:T(2,128)} %noise.1, f32[2,8,1024]{2,1,0:T(8,128)} %probes.1, s32[2,4]{1,0:T(2,128)} %pairs.1), custom_call_target="tpu_custom_call" | custom-call | tf_op jit(solution)/shard_map/pallas_call | solution.py:255
  41.2 0.6 %copy.8 = f32[2,8,1024]{2,1,0:T(8,128)} copy(f32[2,8,1024]{2,1,0:T(8,128)S(1)} %get-tuple-element.4) | data formatting | bytes 131072
  41.8 0.6 %copy.9 = f32[2,128]{1,0:T(2,128)} copy(f32[2,128]{1,0:T(2,128)S(1)} %get-tuple-element.5) | data formatting | bytes 2048

commit v3 on v2

--- a/solution.py
+++ b/solution.py
@@ -18,9 +18,11 @@
 GROUPS = NY * NZ
 LANES = 128
 STRIPS = PTS // LANES
-
-S_COORDS, S_Q, S_D, S_Z, S_ZX, S_P, S_AZ, S_AY = 0, 2, 7, 8, 11, 12, 19, 50
-N_SEMS = 65
+MID = PTS // 2
+HALVES = (slice(0, MID), slice(MID, PTS))
+
+S_COORDS, S_Q, S_D, S_Z, S_ZX, S_P, S_AZ, S_AY, S_T = 0, 2, 7, 8, 11, 12, 13, 14, 15
+N_SEMS = 16
 
 
 def fold(values):
@@ -31,8 +33,8 @@
 
 
 def kernel(
-    coords, noise, probes, pairs, sol, var,
-    cbuf, lane, spread, nv, pv, qbuf, dbuf, qt, k_self, k_pair, k_near, k_far, zf, zb, zr, zx,
+    coords, noise, probes, pair_list, sol, var,
+    pairs, cbuf, lane, spread, nv, pv, qbuf, dbuf, qt, k_self, k_pair, k_near, k_far, zf, zp, zo, zb, zr, zx,
     az, ay, coef, ps, pr, lsem, ssem, rsem, s1, s2, s3,
 ):
     g = lax.axis_index("tiles")
@@ -58,7 +60,7 @@
 
     loads = [
         pltpu.make_async_copy(src, dst, lsem.at[i])
-        for i, (src, dst) in enumerate(((coords, cbuf.at[1]), (probes, pv), (noise, nv)))
+        for i, (src, dst) in enumerate(((coords, cbuf.at[1]), (probes, pv), (noise, nv), (pair_list, pairs)))
     ]
     for load in loads:
         load.start()
@@ -73,11 +75,14 @@
     for device in near:
         signal(barrier, device)
 
-    def fill(block, cols, low=0, high=STRIPS):
+    def in_order(values):
+        return jnp.where(c == 0, values, jnp.concatenate([values[:, MID:], values[:, :MID]], 1))
+
+    def fill(block, cols, low=0, high=STRIPS, strips=range(STRIPS)):
         def step(r, carry):
             at_rows = pl.ds(pl.multiple_of(r * LANES, LANES), LANES)
             px, py = spread[0, at_rows, :], spread[1, at_rows, :]
-            for b in range(STRIPS):
+            for b in strips:
                 cut = slice(b * LANES, (b + 1) * LANES)
                 dx = px - lane[cols, 0:1, cut]
                 dy = py - lane[cols, 1:2, cut]
@@ -98,8 +103,8 @@
     def times(field, block):
         return jnp.dot(field[...], block[...], preferred_element_type=F32)
 
-    for load in loads:
-        load.wait()
+    loads[0].wait()
+    loads[1].wait()
     lane[0] = cbuf[1, c] * 8.0
     for axis in range(2):
         for b in range(STRIPS):
@@ -107,7 +112,7 @@
             spread[axis, cut, :] = jnp.broadcast_to(lane[0, axis : axis + 1, cut], (LANES, LANES)).T
     qbuf[1, c] = pv[...].reshape(2 * HALF, PTS).astype(BF16)
     dbuf[c] = pv[c]
-    lane[1] = cbuf[1, other] * 8.0
+    lane[1] = in_order(cbuf[1, other]) * 8.0
     fill(k_self, 0, 0, 3)
 
     pl.semaphore_wait(barrier, len(near))
@@ -127,7 +132,8 @@
         signal(s1, device)
 
     fill(k_self, 0, 3)
-    fill(k_pair, 1)
+    fill(k_pair, 1, 0, STRIPS // 2, range(STRIPS // 2))
+    fill(k_pair, 1, STRIPS // 2, STRIPS, range(STRIPS // 2, STRIPS))
 
     def by_tile(group):
         first, second = qbuf[group, 0].astype(F32), qbuf[group, 1].astype(F32)
@@ -142,11 +148,20 @@
     sends[2].wait_recv()
     t0, t1 = by_tile(1)
     qt[0] = jnp.where(c == 0, t0, t1).astype(BF16)
-    qt[1] = jnp.where(c == 0, t1, t0).astype(BF16)
-    zf[...] = times(qt.at[0], k_self) + times_rows(qt.at[1], k_pair)
+    qt[1] = in_order(jnp.where(c == 0, t1, t0)).astype(BF16)
+    for h in HALVES:
+        zp[:, h] = times(qt.at[0, :, h], k_pair.at[h, h])
+    zp[...] = in_order(zp[...])
+    to_partner = copy(zp, zo, S_T, near[4])
+    to_partner.start()
+    zf[...] = times(qt.at[0], k_self)
+    for h in HALVES:
+        zf[:, h] += times_rows(qt.at[1, :, h], k_pair.at[h, h])
 
     sends[0].wait_recv()
     sends[1].wait_recv()
+    loads[2].wait()
+    loads[3].wait()
     first_next = 2 * (g + 1)
     low = (pairs[c, 1] >= first_next) | (pairs[c, 2] >= first_next) | (pairs[c, 3] >= first_next)
     lane[2] = jnp.where(low, cbuf[2, c], cbuf[0, other]) * 8.0
@@ -166,7 +181,8 @@
     sends[3].wait_recv()
     noise_row = nv[pl.ds(c, 1), :]
     start = dbuf[...].reshape(CHIP, PTS)
-    image = zf[...] + times_rows(qt.at[2], k_near) + times_rows(qt.at[3], k_far)
+    to_partner.wait_recv()
+    image = zf[...] + zo[...] + times_rows(qt.at[2], k_near) + times_rows(qt.at[3], k_far)
     image = noise_row * start + image * (1.0 / 256.0)
     zf[...] = image
     zb[...] = image.astype(BF16)
@@ -186,16 +202,18 @@
     shares = []
     for j, (dx, dc) in enumerate([(dx, dc) for dx in range(NX) for dc in range(2)][1:]):
         device = at(dx=dx, dc=dc)
-        shares.append(copy(ps.at[device["probe"]], pr.at[j], S_P + j, device))
+        shares.append(copy(ps.at[device["probe"]], pr.at[j], S_P, device))
     for send in shares:
         send.start()
+    all_shares = copy(pr, pr, S_P, near[4])
 
     moments = [fold(products[0]), fold(products[1]), fold(image * image)]
     square = fold(image * (times(zb, k_self) * (1.0 / 256.0) + noise_row * image))
-    to_pair, to_near = times(zb, k_pair), times(zb, k_near)
+    to_near = times(zb, k_near)
+    to_pair = jnp.concatenate([times(zb.at[:, h], k_pair.at[h, h]) for h in HALVES], 1)
     pl.semaphore_wait(s3, 3)
     fields[2].wait_recv()
-    square = square + fold(to_pair * zr[0].astype(F32)) * (1.0 / 256.0)
+    square = square + fold(to_pair * in_order(zr[0].astype(F32))) * (2.0 / 256.0)
     fields[0].wait_recv()
     fields[1].wait_recv()
     across = jnp.where(low, zr[1].astype(F32), zr[2].astype(F32))
@@ -203,17 +221,22 @@
 
     table = jnp.concatenate(moments + [square, jnp.zeros((64, LANES), F32)], 0)
     az[0] = jnp.sum(table.T, axis=0, keepdims=True)
-    along_z = [copy(az.at[0], az.at[i], S_AZ + i - 1, at(dz=i // 2, dc=i % 2)) for i in range(1, 2 * NZ)]
+    along_z = [copy(az.at[0], az.at[i], S_AZ, at(dz=i // 2, dc=i % 2)) for i in range(1, 2 * NZ)]
+    all_z = copy(az.at[pl.ds(1, 2 * NZ - 1)], az.at[pl.ds(1, 2 * NZ - 1)], S_AZ, near[4])
     for i in sorted(range(1, 2 * NZ), key=lambda i: -min(i // 2, NZ - i // 2)):
         along_z[i - 1].start()
-    for send in along_z:
-        send.wait_recv()
+    for send in sends + fields + [to_partner, all_shares]:
+        send.wait_send()
+    all_z.wait_recv()
     ay[0] = jnp.sum(az[...], axis=0)
-    plane = [copy(ay.at[0], ay.at[i], S_AY + i - 1, at(dx=i // NY, dy=i % NY)) for i in range(1, NX * NY)]
+    plane = [copy(ay.at[0], ay.at[i], S_AY, at(dx=i // NY, dy=i % NY)) for i in range(1, NX * NY)]
     for i in sorted(range(1, NX * NY), key=lambda i: -(min(i // NY, NX - i // NY) + min(i % NY, NY - i % NY))):
         plane[i - 1].start()
-    for send in plane:
-        send.wait_recv()
+    all_plane = copy(ay.at[pl.ds(1, NX * NY - 1)], ay.at[pl.ds(1, NX * NY - 1)], S_AY, near[4])
+    all_z.wait_send()
+    fields[3].wait_recv()
+    all_shares.wait_recv()
+    all_plane.wait_recv()
     m0 = jnp.concatenate([jnp.sum(ay[NY * i : NY * (i + 1)], axis=0) for i in range(NX)], 0)
     m1, m2, m3 = (pltpu.roll(m0, LANES - CHIP * i, 1) for i in (1, 2, 3))
     step0 = m0 / m1
@@ -234,11 +257,8 @@
     mine = pl.ds(pl.multiple_of(c * HALF, HALF), HALF)
     alpha_mine = jnp.concatenate([coef[mine, :]] * STRIPS, 1)
     beta_mine = jnp.concatenate([coef[pl.ds(pl.multiple_of(CHIP + c * HALF, HALF), HALF), :]] * STRIPS, 1)
-    fields[3].wait_recv()
     sol[c] = alpha_mine * pv[c] + beta_mine * zf[mine, :]
     sol[other] = alpha_mine * pv[other] + beta_mine * zx[...]
-    for send in shares:
-        send.wait_recv()
     for dc, tile in ((0, c), (1, other)):
         total = jnp.zeros((CHIP, LANES), F32)
         for dx in range(NX):
@@ -246,8 +266,7 @@
             total = total + coef[32 * dx : 32 * dx + CHIP, :] * share[0]
             total = total + coef[32 * dx + CHIP : 32 * dx + 2 * CHIP, :] * share[1]
         var[pl.ds(tile, 1), :] = jnp.sum(total, axis=0, keepdims=True) * (1.0 / PROBES)
-    for send in sends + fields + shares + along_z + plane:
-        send.wait_send()
+    all_plane.wait_send()
 
 
 def shards(coords, noise_var, probes, pair_list):
@@ -258,9 +277,10 @@
             jax.ShapeDtypeStruct(probes.shape, F32),
             jax.ShapeDtypeStruct((2, LANES), F32),
         ),
-        in_specs=[anywhere, anywhere, anywhere, pl.BlockSpec(memory_space=pltpu.SMEM)],
+        in_specs=[anywhere] * 4,
         out_specs=[pl.BlockSpec(memory_space=pltpu.VMEM)] * 2,
         scratch_shapes=[
+            pltpu.SMEM((2, 4), jnp.int32),
             pltpu.VMEM((3, 2, 2, PTS), F32),
             pltpu.VMEM((4, 2, PTS), F32),
             pltpu.VMEM((2, PTS, LANES), F32),
@@ -274,6 +294,8 @@
             pltpu.VMEM((PTS, PTS), BF16),
             pltpu.VMEM((PTS, PTS), BF16),
             pltpu.VMEM((CHIP, PTS), F32),
+            pltpu.VMEM((CHIP, PTS), F32),
+            pltpu.VMEM((CHIP, PTS), F32),
             pltpu.VMEM((CHIP, PTS), BF16),
             pltpu.VMEM((3, CHIP, PTS), BF16),
             pltpu.VMEM((HALF, PTS), F32),
@@ -282,7 +304,7 @@
             pltpu.VMEM((LANES, LANES), F32),
             pltpu.VMEM((8, 2, CHIP, LANES), F32),
             pltpu.VMEM((7, 2, CHIP, LANES), F32),
-            pltpu.SemaphoreType.DMA((3,)),
+            pltpu.SemaphoreType.DMA((4,)),
             pltpu.SemaphoreType.DMA((N_SEMS,)),
             pltpu.SemaphoreType.DMA((N_SEMS,)),
             pltpu.SemaphoreType.REGULAR,

time: 42.6 us -> 39.8 us (0.934)
  Pallas kernels: 40.5 us -> 37.8 us
    pallas_call x1, Pallas kernels: 40.5 us -> 37.8 us  [shards(): pl.pallas_call(kernel, out_shape=(jax.ShapeDtypeStruct(probes.shape, F32)...]
where the time goes in v3:
time: 39.8 us; the launch traced here: 39.7 us
  Pallas kernels  37.8 us (95%)
  local copies, waits for them, and re-layouts  1.19 us (3%)
  between operations  0.64 us (2%)
    pallas_call x1, Pallas kernels, shards(): pl.pallas_call(kernel, out_shape=(jax.ShapeDtypeStruct(probes.shape, F32)...  37.8 us
    unnamed x2, local copies, waits for them, and re-layouts  1.19 us

profile of v3, /device:TPU:1, one launch (start us, length us, event | category | flops | bytes accessed | tf_op | source)
XLA Modules:
  0.0 39.7 jit_solution(17475979831767442756)
XLA Ops:
  0.6 37.8 %shard_map.59 = (f32[2,8,1024]{2,1,0:T(8,128)S(1)}, f32[2,128]{1,0:T(2,128)S(1)}) custom-call(f32[2,2,1024]{2,1,0:T(2,128)} %coords.1, f32[2,1024]{1,0:T(2,128)} %noise.1, f32[2,8,1024]{2,1,0:T(8,128)} %probes.1, s32[2,4]{1,0:T(2,128)} %pair_list.1), custom_call_target="tpu_custom_call" | custom-call | tf_op jit(solution)/shard_map/pallas_call | solution.py:274
  38.5 0.6 %copy.8 = f32[2,8,1024]{2,1,0:T(8,128)} copy(f32[2,8,1024]{2,1,0:T(8,128)S(1)} %get-tuple-element.4) | data formatting | bytes 131072
  39.1 0.6 %copy.9 = f32[2,128]{1,0:T(2,128)} copy(f32[2,128]{1,0:T(2,128)S(1)} %get-tuple-element.5) | data formatting | bytes 2048

commit v4 on v3

--- a/solution.py
+++ b/solution.py
@@ -18,6 +18,7 @@
 GROUPS = NY * NZ
 LANES = 128
 STRIPS = PTS // LANES
+WIDE = 2 * LANES
 MID = PTS // 2
 HALVES = (slice(0, MID), slice(MID, PTS))
 
@@ -35,7 +36,7 @@
 def kernel(
     coords, noise, probes, pair_list, sol, var,
     pairs, cbuf, lane, spread, nv, pv, qbuf, dbuf, qt, k_self, k_pair, k_near, k_far, zf, zp, zo, zb, zr, zx,
-    az, ay, coef, ps, pr, lsem, ssem, rsem, s1, s2, s3,
+    az, ay, coef, ps, pr, lsem, ssem, rsem, s1, s2, s3, x1, x2, x3,
 ):
     g = lax.axis_index("tiles")
     k = lax.axis_index("probe")
@@ -78,16 +79,16 @@
     def in_order(values):
         return jnp.where(c == 0, values, jnp.concatenate([values[:, MID:], values[:, :MID]], 1))
 
-    def fill(block, cols, low=0, high=STRIPS, strips=range(STRIPS)):
+    def fill(block, cols, low=0, high=STRIPS, strips=range(PTS // WIDE)):
         def step(r, carry):
             at_rows = pl.ds(pl.multiple_of(r * LANES, LANES), LANES)
-            px, py = spread[0, at_rows, :], spread[1, at_rows, :]
+            px = jnp.concatenate([spread[0, at_rows, :]] * 2, 1)
+            py = jnp.concatenate([spread[1, at_rows, :]] * 2, 1)
             for b in strips:
-                cut = slice(b * LANES, (b + 1) * LANES)
+                cut = slice(b * WIDE, (b + 1) * WIDE)
                 dx = px - lane[cols, 0:1, cut]
                 dy = py - lane[cols, 1:2, cut]
-                square = jnp.maximum(dx * dx + dy * dy, 1e-30)
-                s4 = square * lax.rsqrt(square)
+                s4 = pltpu.reciprocal(lax.rsqrt(dx * dx + dy * dy), approx=True)
                 m = jnp.maximum(4.0 - s4, 0.0)
                 m = m * m
                 block[at_rows, cut] = ((m * m) * (s4 + 1.0)).astype(BF16)
@@ -128,12 +129,12 @@
     ]
     for send in sends:
         send.start()
-    for device in (at(dz=1), at(dz=-1), at(dy=-1), at(dx=-1), at(dx=1)):
+    for device in (at(dz=1), at(dz=-1)):
         signal(s1, device)
 
     fill(k_self, 0, 3)
-    fill(k_pair, 1, 0, STRIPS // 2, range(STRIPS // 2))
-    fill(k_pair, 1, STRIPS // 2, STRIPS, range(STRIPS // 2, STRIPS))
+    fill(k_pair, 1, 0, STRIPS // 2, range(MID // WIDE))
+    fill(k_pair, 1, STRIPS // 2, STRIPS, range(MID // WIDE, PTS // WIDE))
 
     def by_tile(group):
         first, second = qbuf[group, 0].astype(F32), qbuf[group, 1].astype(F32)
@@ -142,8 +143,8 @@
             jnp.concatenate([first[HALF:], second[HALF:]], 0),
         )
 
-    pl.semaphore_wait(s1, 5)
-    for device in (at(dz=2), at(dz=-2), at(dx=-1), at(dx=1)):
+    pl.semaphore_wait(s1, 2)
+    for device in (at(dz=2), at(dz=-2)):
         signal(s2, device)
     sends[2].wait_recv()
     t0, t1 = by_tile(1)
@@ -168,8 +169,8 @@
     lane[3] = jnp.where(low, cbuf[2, other], cbuf[0, c]) * 8.0
     fill(k_near, 2)
 
-    pl.semaphore_wait(s2, 4)
-    for device in (at(dz=4), at(dz=-4), at(dx=-1)):
+    pl.semaphore_wait(s2, 2)
+    for device in (at(dz=4), at(dz=-4)):
         signal(s3, device)
     fill(k_far, 3)
     for send in sends[4:]:
@@ -193,12 +194,38 @@
         copy(zb, zr.at[0], S_Z + 2, near[4]),
         copy(zf.at[pl.ds(pl.multiple_of(other * HALF, HALF), HALF), :], zx, S_ZX, near[4]),
     ]
-    for send in fields:
+    for send in fields[:3]:
         send.start()
+    for device in (at(dy=-1), at(dx=-1), at(dx=1)):
+        signal(x1, device)
     products = (start * start, start * image)
+    moments = [fold(products[0]), fold(products[1]), fold(image * image)]
+    square = fold(image * (times(zb, k_self) * (1.0 / 256.0) + noise_row * image))
+    to_near = times(zb, k_near)
+    to_pair = jnp.concatenate([times(zb.at[:, h], k_pair.at[h, h]) for h in HALVES], 1)
+    pl.semaphore_wait(s3, 2)
+    fields[2].wait_recv()
+    square = square + fold(to_pair * in_order(zr[0].astype(F32))) * (2.0 / 256.0)
+    fields[0].wait_recv()
+    fields[1].wait_recv()
+    across = jnp.where(low, zr[1].astype(F32), zr[2].astype(F32))
+    square = square + fold(to_near * across) * (2.0 / 256.0)
+
+    table = jnp.concatenate(moments + [square, jnp.zeros((64, LANES), F32)], 0)
+    az[0] = jnp.sum(table.T, axis=0, keepdims=True)
+    along_z = [copy(az.at[0], az.at[i], S_AZ, at(dz=i // 2, dc=i % 2)) for i in range(1, 2 * NZ)]
+    all_z = copy(az.at[pl.ds(1, 2 * NZ - 1)], az.at[pl.ds(1, 2 * NZ - 1)], S_AZ, near[4])
+    for i in sorted(range(1, 2 * NZ), key=lambda i: -min(i // 2, NZ - i // 2)):
+        along_z[i - 1].start()
+    pl.semaphore_wait(x1, 3)
+    for device in (at(dx=-1), at(dx=1)):
+        signal(x2, device)
     for j in range(STRIPS):
         for i in range(2):
             ps[j, i] = products[i][:, j * LANES : (j + 1) * LANES]
+    fields[3].start()
+    pl.semaphore_wait(x2, 2)
+    signal(x3, at(dx=-1))
     shares = []
     for j, (dx, dc) in enumerate([(dx, dc) for dx in range(NX) for dc in range(2)][1:]):
         device = at(dx=dx, dc=dc)
@@ -207,26 +234,9 @@
         send.start()
     all_shares = copy(pr, pr, S_P, near[4])
 
-    moments = [fold(products[0]), fold(products[1]), fold(image * image)]
-    square = fold(image * (times(zb, k_self) * (1.0 / 256.0) + noise_row * image))
-    to_near = times(zb, k_near)
-    to_pair = jnp.concatenate([times(zb.at[:, h], k_pair.at[h, h]) for h in HALVES], 1)
-    pl.semaphore_wait(s3, 3)
-    fields[2].wait_recv()
-    square = square + fold(to_pair * in_order(zr[0].astype(F32))) * (2.0 / 256.0)
-    fields[0].wait_recv()
-    fields[1].wait_recv()
-    across = jnp.where(low, zr[1].astype(F32), zr[2].astype(F32))
-    square = square + fold(to_near * across) * (2.0 / 256.0)
-
-    table = jnp.concatenate(moments + [square, jnp.zeros((64, LANES), F32)], 0)
-    az[0] = jnp.sum(table.T, axis=0, keepdims=True)
-    along_z = [copy(az.at[0], az.at[i], S_AZ, at(dz=i // 2, dc=i % 2)) for i in range(1, 2 * NZ)]
-    all_z = copy(az.at[pl.ds(1, 2 * NZ - 1)], az.at[pl.ds(1, 2 * NZ - 1)], S_AZ, near[4])
-    for i in sorted(range(1, 2 * NZ), key=lambda i: -min(i // 2, NZ - i // 2)):
-        along_z[i - 1].start()
     for send in sends + fields + [to_partner, all_shares]:
         send.wait_send()
+    pl.semaphore_wait(x3, 1)
     all_z.wait_recv()
     ay[0] = jnp.sum(az[...], axis=0)
     plane = [copy(ay.at[0], ay.at[i], S_AY, at(dx=i // NY, dy=i % NY)) for i in range(1, NX * NY)]
@@ -310,6 +320,9 @@
             pltpu.SemaphoreType.REGULAR,
             pltpu.SemaphoreType.REGULAR,
             pltpu.SemaphoreType.REGULAR,
+            pltpu.SemaphoreType.REGULAR,
+            pltpu.SemaphoreType.REGULAR,
+            pltpu.SemaphoreType.REGULAR,
         ],
         compiler_params=pltpu.CompilerParams(
             collective_id=0, has_side_effects=True, vmem_limit_bytes=32 << 20

time: 39.8 us -> 39.3 us (0.987)
  Pallas kernels: 37.8 us -> 37.3 us
    pallas_call x1, Pallas kernels: 37.8 us -> 37.3 us  [shards(): pl.pallas_call(kernel, out_shape=(jax.ShapeDtypeStruct(probes.shape, F32)...]
where the time goes in v4:
time: 39.3 us; the launch traced here: 39.1 us
  Pallas kernels  37.3 us (95%)
  local copies, waits for them, and re-layouts  1.19 us (3%)
  between operations  0.64 us (2%)
    pallas_call x1, Pallas kernels, shards(): pl.pallas_call(kernel, out_shape=(jax.ShapeDtypeStruct(probes.shape, F32)...  37.3 us
    unnamed x2, local copies, waits for them, and re-layouts  1.19 us

profile of v4, /device:TPU:1, one launch (start us, length us, event | category | flops | bytes accessed | tf_op | source)
XLA Modules:
  0.0 39.1 jit_solution(17052339365272845198)
XLA Ops:
  0.6 37.3 %shard_map.59 = (f32[2,8,1024]{2,1,0:T(8,128)S(1)}, f32[2,128]{1,0:T(2,128)S(1)}) custom-call(f32[2,2,1024]{2,1,0:T(2,128)} %coords.1, f32[2,1024]{1,0:T(2,128)} %noise.1, f32[2,8,1024]{2,1,0:T(8,128)} %probes.1, s32[2,4]{1,0:T(2,128)} %pair_list.1), custom_call_target="tpu_custom_call" | custom-call | tf_op jit(solution)/shard_map/pallas_call | solution.py:284
  37.9 0.6 %copy.8 = f32[2,8,1024]{2,1,0:T(8,128)} copy(f32[2,8,1024]{2,1,0:T(8,128)S(1)} %get-tuple-element.4) | data formatting | bytes 131072
  38.6 0.6 %copy.9 = f32[2,128]{1,0:T(2,128)} copy(f32[2,128]{1,0:T(2,128)S(1)} %get-tuple-element.5) | data formatting | bytes 2048

commit v5 on v4

--- a/solution.py
+++ b/solution.py
@@ -19,6 +19,8 @@
 LANES = 128
 STRIPS = PTS // LANES
 WIDE = 2 * LANES
+BAND = 256
+BANDS = PTS // BAND
 MID = PTS // 2
 HALVES = (slice(0, MID), slice(MID, PTS))
 
@@ -79,9 +81,9 @@
     def in_order(values):
         return jnp.where(c == 0, values, jnp.concatenate([values[:, MID:], values[:, :MID]], 1))
 
-    def fill(block, cols, low=0, high=STRIPS, strips=range(PTS // WIDE)):
+    def fill(block, cols, low=0, high=BANDS, strips=range(PTS // WIDE)):
         def step(r, carry):
-            at_rows = pl.ds(pl.multiple_of(r * LANES, LANES), LANES)
+            at_rows = pl.ds(pl.multiple_of(r * BAND, BAND), BAND)
             px = jnp.concatenate([spread[0, at_rows, :]] * 2, 1)
             py = jnp.concatenate([spread[1, at_rows, :]] * 2, 1)
             for b in strips:
@@ -114,7 +116,7 @@
     qbuf[1, c] = pv[...].reshape(2 * HALF, PTS).astype(BF16)
     dbuf[c] = pv[c]
     lane[1] = in_order(cbuf[1, other]) * 8.0
-    fill(k_self, 0, 0, 3)
+    fill(k_self, 0, 0, 1)
 
     pl.semaphore_wait(barrier, len(near))
     sends = [
@@ -127,14 +129,16 @@
         copy(qbuf.at[1, c], qbuf.at[2, c], S_Q + 3, near[2]),
         copy(qbuf.at[1, c], qbuf.at[2, c], S_Q + 4, near[3]),
     ]
-    for send in sends:
+    for send in sends[:4]:
         send.start()
     for device in (at(dz=1), at(dz=-1)):
         signal(s1, device)
 
-    fill(k_self, 0, 3)
-    fill(k_pair, 1, 0, STRIPS // 2, range(MID // WIDE))
-    fill(k_pair, 1, STRIPS // 2, STRIPS, range(MID // WIDE, PTS // WIDE))
+    fill(k_self, 0, 1)
+    for send in sends[4:]:
+        send.start()
+    fill(k_pair, 1, 0, BANDS // 2, range(MID // WIDE))
+    fill(k_pair, 1, BANDS // 2, BANDS, range(MID // WIDE, PTS // WIDE))
 
     def by_tile(group):
         first, second = qbuf[group, 0].astype(F32), qbuf[group, 1].astype(F32)

time: 39.3 us -> 39 us (level)
  no operation moved by 1% of the time
where the time goes in v5:
time: 39 us; the launch traced here: 38.8 us
  Pallas kernels  37 us (95%)
  local copies, waits for them, and re-layouts  1.19 us (3%)
  between operations  0.64 us (2%)
    pallas_call x1, Pallas kernels, shards(): pl.pallas_call(kernel, out_shape=(jax.ShapeDtypeStruct(probes.shape, F32)...  37 us
    unnamed x2, local copies, waits for them, and re-layouts  1.19 us

profile of v5, /device:TPU:1, one launch (start us, length us, event | category | flops | bytes accessed | tf_op | source)
XLA Modules:
  0.0 38.8 jit_solution(1507241280810240796)
XLA Ops:
  0.6 37.0 %shard_map.59 = (f32[2,8,1024]{2,1,0:T(8,128)S(1)}, f32[2,128]{1,0:T(2,128)S(1)}) custom-call(f32[2,2,1024]{2,1,0:T(2,128)} %coords.1, f32[2,1024]{1,0:T(2,128)} %noise.1, f32[2,8,1024]{2,1,0:T(8,128)} %probes.1, s32[2,4]{1,0:T(2,128)} %pair_list.1), custom_call_target="tpu_custom_call" | custom-call | tf_op jit(solution)/shard_map/pallas_call | solution.py:288
  37.6 0.6 %copy.8 = f32[2,8,1024]{2,1,0:T(8,128)} copy(f32[2,8,1024]{2,1,0:T(8,128)S(1)} %get-tuple-element.4) | data formatting | bytes 131072
  38.3 0.6 %copy.9 = f32[2,128]{1,0:T(2,128)} copy(f32[2,128]{1,0:T(2,128)S(1)} %get-tuple-element.5) | data formatting | bytes 2048

commit v6 on v5

--- a/solution.py
+++ b/solution.py
@@ -37,7 +37,7 @@
 
 def kernel(
     coords, noise, probes, pair_list, sol, var,
-    pairs, cbuf, lane, spread, nv, pv, qbuf, dbuf, qt, k_self, k_pair, k_near, k_far, zf, zp, zo, zb, zr, zx,
+    pairs, cbuf, lane, spread, nv, pv, qbuf, dbuf, qt, k_self, k_pair, k_nb, qn, zf, zp, zo, zb, zr, zx,
     az, ay, coef, ps, pr, lsem, ssem, rsem, s1, s2, s3, x1, x2, x3,
 ):
     g = lax.axis_index("tiles")
@@ -171,6 +171,7 @@
     low = (pairs[c, 1] >= first_next) | (pairs[c, 2] >= first_next) | (pairs[c, 3] >= first_next)
     lane[2] = jnp.where(low, cbuf[2, c], cbuf[0, other]) * 8.0
     lane[3] = jnp.where(low, cbuf[2, other], cbuf[0, c]) * 8.0
+    k_near, k_far = k_nb.at[:, :PTS], k_nb.at[:, PTS:]
     fill(k_near, 2)
 
     pl.semaphore_wait(s2, 2)
@@ -181,13 +182,13 @@
         send.wait_recv()
     p0, p1 = by_tile(0)
     n0, n1 = by_tile(2)
-    qt[2] = jnp.where(low, jnp.where(c == 0, n0, n1), jnp.where(c == 0, p1, p0)).astype(BF16)
-    qt[3] = jnp.where(low, jnp.where(c == 0, n1, n0), jnp.where(c == 0, p0, p1)).astype(BF16)
+    qn[:, :PTS] = jnp.where(low, jnp.where(c == 0, n0, n1), jnp.where(c == 0, p1, p0)).astype(BF16)
+    qn[:, PTS:] = jnp.where(low, jnp.where(c == 0, n1, n0), jnp.where(c == 0, p0, p1)).astype(BF16)
     sends[3].wait_recv()
     noise_row = nv[pl.ds(c, 1), :]
     start = dbuf[...].reshape(CHIP, PTS)
     to_partner.wait_recv()
-    image = zf[...] + zo[...] + times_rows(qt.at[2], k_near) + times_rows(qt.at[3], k_far)
+    image = zf[...] + zo[...] + times_rows(qn, k_nb)
     image = noise_row * start + image * (1.0 / 256.0)
     zf[...] = image
     zb[...] = image.astype(BF16)
@@ -302,11 +303,11 @@
             pltpu.VMEM((2, HALF, PTS), F32),
             pltpu.VMEM((3, 2, 2 * HALF, PTS), BF16),
             pltpu.VMEM((2, HALF, PTS), F32),
-            pltpu.VMEM((4, CHIP, PTS), BF16),
+            pltpu.VMEM((2, CHIP, PTS), BF16),
             pltpu.VMEM((PTS, PTS), BF16),
             pltpu.VMEM((PTS, PTS), BF16),
-            pltpu.VMEM((PTS, PTS), BF16),
-            pltpu.VMEM((PTS, PTS), BF16),
+            pltpu.VMEM((PTS, 2 * PTS), BF16),
+            pltpu.VMEM((CHIP, 2 * PTS), BF16),
             pltpu.VMEM((CHIP, PTS), F32),
             pltpu.VMEM((CHIP, PTS), F32),
             pltpu.VMEM((CHIP, PTS), F32),

time: 39 us -> 39 us (level)
  no operation moved by 1% of the time
where the time goes in v6:
time: 39 us; the launch traced here: 38.8 us
  Pallas kernels  37 us (95%)
  local copies, waits for them, and re-layouts  1.19 us (3%)
  between operations  0.64 us (2%)
    pallas_call x1, Pallas kernels, shards(): pl.pallas_call(kernel, out_shape=(jax.ShapeDtypeStruct(probes.shape, F32)...  37 us
    unnamed x2, local copies, waits for them, and re-layouts  1.19 us

profile of v6, /device:TPU:1, one launch (start us, length us, event | category | flops | bytes accessed | tf_op | source)
XLA Modules:
  0.0 38.8 jit_solution(389792164801442463)
XLA Ops:
  0.6 37.0 %shard_map.59 = (f32[2,8,1024]{2,1,0:T(8,128)S(1)}, f32[2,128]{1,0:T(2,128)S(1)}) custom-call(f32[2,2,1024]{2,1,0:T(2,128)} %coords.1, f32[2,1024]{1,0:T(2,128)} %noise.1, f32[2,8,1024]{2,1,0:T(8,128)} %probes.1, s32[2,4]{1,0:T(2,128)} %pair_list.1), custom_call_target="tpu_custom_call" | custom-call | tf_op jit(solution)/shard_map/pallas_call | solution.py:289
  37.6 0.6 %copy.8 = f32[2,8,1024]{2,1,0:T(8,128)} copy(f32[2,8,1024]{2,1,0:T(8,128)S(1)} %get-tuple-element.4) | data formatting | bytes 131072
  38.3 0.6 %copy.9 = f32[2,128]{1,0:T(2,128)} copy(f32[2,128]{1,0:T(2,128)S(1)} %get-tuple-element.5) | data formatting | bytes 2048
